TPU v7x, 512 devices: a whole 4x8x8 slice. The times are simulated.
512 devices in a mesh: ctx: 64 (over y_lo, z, x), tp: 8 (over y_hi, core).
Axes of the slice: x: 4, y: 8 (y_hi: 4, y_lo: 2; y = y_hi * 2 + y_lo), z: 8, core: 2. Of those that a mesh axis runs over, the one named last changes fastest.
Arguments:
- queries: bfloat16 [16384, 8192], P('ctx', 'tp'), may hold values from -128 to 128
- cotangent: bfloat16 [16384, 8192], P('ctx', 'tp'), may hold values from -96 to 96
- image_keys: bfloat16 [64, 64, 1024], P('ctx', None, 'tp'), may hold values from -8 to 8
- image_values: bfloat16 [64, 64, 1024], P('ctx', None, 'tp'), may hold values from -6 to 6
- attn_gate: float32 [1], replicated, may hold values from 0.4 to 1.5
- block_mask: int32 [128, 64], P('ctx'), may hold values from 0 to 1, as said below
- image_owner: int32 [64], replicated, may hold values from 0 to 63, each once
Outputs:
- query_grad: bfloat16 [16384, 8192], P('ctx', 'tp')
- key_grad: bfloat16 [64, 64, 1024], P('ctx', None, 'tp')
- value_grad: bfloat16 [64, 64, 1024], P('ctx', None, 'tp')
- gate_grad: float32 [1], replicated
Inputs may be any that keep to these rules, and one draw needn't show every extreme that they name: `block_mask`: every text block reads at least one image; the 2 blocks of one index of ctx together read exactly 32 distinct images.
All inputs are finite; a program needn't handle non-finite values.
Results may differ from a plain program's by a relative error of at most 0.02.
Values may be sent and summed in bfloat16 or wider, within the bound.
A program may use at most 64 MiB of HBM per device.

v0:
```python
import math
import jax
import jax.numpy as jnp
from jax import lax
from jax.sharding import PartitionSpec as P

HD = 128
BLK = 128


def per_device(queries, cotangent, image_keys, image_values, attn_gate, block_mask, image_owner):
    tok_dev = queries.shape[0]
    local_kv = image_keys.shape[2] // HD
    local_heads = queries.shape[1] // HD
    groups = local_heads // local_kv
    img_tok = image_keys.shape[1]
    inv_root = 1.0 / math.sqrt(HD)
    read_most = lax.axis_size("ctx") // 2
    gathered_keys, gathered_values = (
        lax.all_gather(image_keys, "ctx", axis=0, tiled=True),
        lax.all_gather(image_values, "ctx", axis=0, tiled=True),
    )
    n_images = gathered_keys.shape[0]
    read_any = jnp.max(block_mask, axis=0)
    ranking = read_any * (2 * n_images) + (n_images - 1 - jnp.arange(n_images, dtype=jnp.int32))
    top_vals, image_ids = lax.top_k(ranking, read_most)
    is_read = read_any[image_ids] > 0
    slot_ids = image_owner[image_ids]
    block_keep = (block_mask[:, image_ids] > 0) & is_read[None, :]
    keep_mask = jnp.repeat(jnp.repeat(block_keep, BLK, axis=0), img_tok, axis=1)
    key_rows = jnp.take(gathered_keys, slot_ids, axis=0).reshape(read_most * img_tok, local_kv, HD)
    value_rows = jnp.take(gathered_values, slot_ids, axis=0).reshape(
        read_most * img_tok, local_kv, HD
    )
    query_heads = queries.reshape(tok_dev, local_kv, groups, HD).transpose(2, 0, 1, 3)
    cot_heads = cotangent.reshape(tok_dev, local_kv, groups, HD).transpose(2, 0, 1, 3)
    gate_value = jnp.tanh(attn_gate[0])

    def head_step(state_in, head_inputs):
        key_acc, value_acc, gate_acc = state_in
        query_one, cot_one = head_inputs
        scores = (
            jnp.einsum("tkd,skd->kts", query_one, key_rows, preferred_element_type=jnp.float32)
            * inv_root
        )
        scores = jnp.where(keep_mask, scores, -1e30)
        row_max = jnp.max(scores, axis=-1, keepdims=True)
        exp_terms = jnp.where(keep_mask, jnp.exp(scores - row_max), 0.0)
        prob_full = exp_terms / jnp.sum(exp_terms, axis=-1, keepdims=True)
        prob_half = prob_full.astype(jnp.bfloat16)
        attended = jnp.einsum(
            "kts,skd->tkd", prob_half, value_rows, preferred_element_type=jnp.float32
        )
        cot_f = cot_one.astype(jnp.float32)
        gate_part = jnp.sum(cot_f * attended)
        attn_grad = (gate_value * cot_f).astype(jnp.bfloat16)
        prob_grad = jnp.einsum(
            "tkd,skd->kts", attn_grad, value_rows, preferred_element_type=jnp.float32
        )
        row_delta = jnp.sum(attn_grad.astype(jnp.float32) * attended, axis=-1).T
        score_grad = (prob_full * (prob_grad - row_delta[:, :, None]) * inv_root).astype(
            jnp.bfloat16
        )
        query_grad = jnp.einsum(
            "kts,skd->tkd", score_grad, key_rows, preferred_element_type=jnp.float32
        ).astype(jnp.bfloat16)
        key_acc = key_acc + jnp.einsum(
            "kts,tkd->skd", score_grad, query_one, preferred_element_type=jnp.float32
        )
        value_acc = value_acc + jnp.einsum(
            "kts,tkd->skd", prob_half, attn_grad, preferred_element_type=jnp.float32
        )
        return ((key_acc, value_acc, gate_acc + gate_part), query_grad)

    zero_grads = jnp.zeros((read_most * img_tok, local_kv, HD), jnp.float32)
    init_state = (zero_grads, zero_grads, jnp.zeros((), jnp.float32))
    (key_acc, value_acc, gate_acc), head_grads = lax.scan(
        head_step, init_state, (query_heads, cot_heads)
    )
    query_grad = head_grads.transpose(1, 2, 0, 3).reshape(tok_dev, local_heads * HD)
    stacked = jnp.concatenate(
        [
            key_acc.reshape(read_most, img_tok, local_kv * HD),
            value_acc.reshape(read_most, img_tok, local_kv * HD),
        ],
        axis=-1,
    )
    stacked = jnp.where(is_read[:, None, None], stacked, 0.0)
    buffer = (
        jnp.zeros((n_images, img_tok, 2 * local_kv * HD), jnp.float32).at[slot_ids].add(stacked)
    )
    received = lax.all_to_all(buffer, "ctx", split_axis=0, concat_axis=0, tiled=True)
    summed = jnp.sum(received, axis=0, keepdims=True)
    key_grad = summed[:, :, : local_kv * HD].astype(jnp.bfloat16)
    value_grad = summed[:, :, local_kv * HD :].astype(jnp.bfloat16)
    gate_total = lax.psum(gate_acc, ("ctx", "tp"))
    term_count = tok_dev * lax.axis_size("ctx") * local_heads * lax.axis_size("tp") * HD
    gate_grad = ((1.0 - gate_value * gate_value) * gate_total / math.sqrt(term_count)).reshape(1)
    return (query_grad, key_grad, value_grad, gate_grad)


def solution(mesh):
    in_specs = (
        P("ctx", "tp"),
        P("ctx", "tp"),
        P("ctx", None, "tp"),
        P("ctx", None, "tp"),
        P(),
        P("ctx", None),
        P(),
    )
    out_specs = (P("ctx", "tp"), P("ctx", None, "tp"), P("ctx", None, "tp"), P())
    return jax.shard_map(
        per_device, mesh=mesh, in_specs=in_specs, out_specs=out_specs, check_vma=False
    )
```

profile of v0, /device:TPU:1, one launch (start us, length us, event | category | flops | bytes accessed | tf_op | source)
XLA Modules:
  0.0 885.6 jit_solution(12151461978923027463)
XLA Ops:
  10.9 2.0 top_k.11
  15.1 1.2 copy.35
  17.4 253.3 %all-gather.5.cloned.1.call-done = bf16[64,64,128]{2,1,0:T(8,128)(2,1)} async-done(((bf16[1,64,128]{2,1,0:T(8,128)(2,1)}), bf16[64,64,128]{2,1,0:T(8,128)(2,1)}) %all-gather.5.cloned.1.call-update) | async-done | bytes 1048592 | tf_op jit(solution)/shard_map/all_gather | solution.py:21
  270.7 1.9 gather_fusion.4
  272.6 297.7 %all-gather.3.cloned.1.call-done = bf16[64,64,128]{2,1,0:T(8,128)(2,1)} async-done(((bf16[1,64,128]{2,1,0:T(8,128)(2,1)}), bf16[64,64,128]{2,1,0:T(8,128)(2,1)}) %all-gather.3.cloned.1.call-update) | async-done | bytes 1048592 | tf_op jit(solution)/shard_map/all_gather | solution.py:20
  570.4 1.9 gather_fusion.3
  572.4 92.9 %while.17 = (s32[]{:T(128)}, f32[2048,1,128]{0,2,1:T(8,128)}, f32[2048,1,128]{0,2,1:T(8,128)}, f32[]{:T(128)}, bf16[8,256,1,128]{3,1,2,0:T(8,128)(2,1)}, /*index...) while((s32[]{:T(128)}, f32[2048,1,128]{0,2,1:T(8,128)}, ...), condition=%wide.region_7.9_spmd.clone, body=%wide.region_2.8_spmd.clone.sunk | while | flops 814710016 | bytes 48644448 | solution.py:77
  575.2 1.9 fusion.68
  577.8 1.4 fusion.69
  579.3 1.4 fusion.71
  580.7 1.1 fusion.72
  581.8 1.3 fusion.70
  586.8 1.9 fusion.68
  589.4 1.4 fusion.69
  590.9 1.4 fusion.71
  593.4 1.3 fusion.70
  598.4 1.9 fusion.68
  601.0 1.4 fusion.69
  602.5 1.4 fusion.71
  605.0 1.3 fusion.70
  610.1 1.9 fusion.68
  612.7 1.4 fusion.69
  614.1 1.4 fusion.71
  616.6 1.3 fusion.70
  621.7 1.9 fusion.68
  624.3 1.4 fusion.69
  625.7 1.4 fusion.71
  628.2 1.3 fusion.70
  633.3 1.9 fusion.68
  635.9 1.4 fusion.69
  637.3 1.4 fusion.71
  639.8 1.3 fusion.70
  644.9 1.9 fusion.68
  647.5 1.4 fusion.69
  649.0 1.4 fusion.71
  651.4 1.3 fusion.70
  656.5 1.9 fusion.68
  659.1 1.4 fusion.69
  660.6 1.4 fusion.71
  663.1 1.3 fusion.70
  665.3 1.6 copy.40
  667.0 1.3 copy.41
  668.3 1.4 maximum_select_fusion
  669.8 2.5 broadcast_in_dim.68
  672.2 6.4 scatter_fusion
  678.6 7.4 all-to-all-start
  686.0 186.7 %psum.7 = f32[]{:T(128)} all-reduce(f32[]{:T(128)} %get-tuple-element.72), channel_id=1, replica_groups=mesh['ctx'=64,'tp'=8] {'ctx','tp'}, use_global_device_ids=true, to_apply=%region_10.12 | all-reduce | flops 1 | bytes 8 | tf_op jit(solution)/shard_map/psum | solution.py:96
  874.6 2.4 reduce_sum.36
  (181 shorter events, 45.7 us)
Async XLA Ops:
  7.2 6.5 copy-start
  7.2 9.2 %copy-start.8 = (bf16[256,1024]{1,0:T(8,128)(2,1)S(1)}, bf16[256,1024]{1,0:T(8,128)(2,1)}, u32[]{:S(2)}) copy-start(bf16[256,1024]{1,0:T(8,128)(2,1)} %param.12) | copy-start | bytes 1572868
  7.2 263.5 %all-gather.5.cloned.1.call-start = ((), (), s32[]{:S(2)}) async-start(), calls=%async_computation.2 | async-start | bytes 1064960 | tf_op jit(solution)/shard_map/all_gather | solution.py:21
  7.9 562.4 %all-gather.3.cloned.1.call-start = ((), (), s32[]{:S(2)}) async-start(), calls=%async_computation.1 | async-start | bytes 1064960 | tf_op jit(solution)/shard_map/all_gather | solution.py:20
  572.4 1.4 copy-start.6
  577.8 1.5 copy-start.1
  579.3 2.5 copy-start.4
  580.7 2.4 copy-start.2
  580.7 3.4 copy-start.7
  584.0 1.4 copy-start.6
  589.4 1.5 copy-start.1
  590.9 2.5 copy-start.4
  592.3 2.4 copy-start.2
  592.3 3.4 copy-start.7
  595.7 1.4 copy-start.6
  601.0 1.5 copy-start.1
  602.5 2.5 copy-start.4
  603.9 2.4 copy-start.2
  603.9 3.4 copy-start.7
  606.3 1.0 copy-start.5
  607.3 1.4 copy-start.6
  612.6 1.5 copy-start.1
  614.1 2.5 copy-start.4
  615.5 2.4 copy-start.2
  615.5 3.4 copy-start.7
  618.9 1.4 copy-start.6
  624.3 1.5 copy-start.1
  625.7 2.5 copy-start.4
  627.1 2.4 copy-start.2
  627.1 3.4 copy-start.7
  630.5 1.4 copy-start.6
  635.9 1.5 copy-start.1
  637.3 2.5 copy-start.4
  638.7 2.4 copy-start.2
  638.7 3.4 copy-start.7
  642.1 1.4 copy-start.6
  647.5 1.5 copy-start.1
  649.0 2.5 copy-start.4
  650.3 2.4 copy-start.2
  650.4 3.4 copy-start.7
  653.7 1.4 copy-start.6
  659.1 1.5 copy-start.1
  660.6 2.5 copy-start.4
  662.0 2.4 copy-start.2
  662.0 3.4 copy-start.7
  665.3 1.6 copy-start.3
  678.6 194.1 %copy-start.9 = (bf16[8,256,1,128]{3,1,2,0:T(8,128)(2,1)S(1)}, bf16[8,256,1,128]{3,1,2,0:T(8,128)(2,1)}, u32[]{:S(2)}) copy-start(bf16[8,256,1,128]{3,1,2,0:T(8,128)(2,1)} %get-tuple-element.69) | copy-start | bytes 1572868
  678.6 196.0 %all-to-all-start = ((f32[64,64,256]{2,1,0:T(8,128)}), f32[64,64,256]{2,1,0:T(8,128)}, u32[]{:S(2)}, u32[]{:S(2)}) async-start(f32[64,64,256]{2,1,0:T(8,128)} %scatter_fusion), calls=%async_computation | async-start | bytes 8388608 | tf_op jit(solution)/shard_map/all_to_all | solution.py:92
  (7 other events, 6.9 us)
Sparse Core Ops, SparseCore 0:
  10.1 260.5 all-gather.4
  272.8 297.4 all-gather.2
where the time goes:
time: 887 us; the launch traced here: 886 us
  waiting for transfers between devices  552 us (62%)
  blocking collectives  187 us (21%)
  matrix products  61.8 us (7%)
  local copies, waits for them, and re-layouts  30.3 us (3%)
  other arithmetic  24.2 us (3%)
  between operations  16.7 us (2%)
    all_gather x1, waiting for transfers between devices, per_device(): lax.all_gather(image_keys, 'ctx', axis=0, tiled=True)  298 us
    all_gather x1, waiting for transfers between devices, per_device(): lax.all_gather(image_values, 'ctx', axis=0, tiled=True)  253 us
    psum x1, blocking collectives, per_device(): gate_total = lax.psum(gate_acc, ('ctx', 'tp'))  187 us
  transfers between devices with their start and end apart: 3, of which 2 were waited for; matrix products, arithmetic and copies ran while one was open for 1% of the time, Pallas kernels for 0%

commit v1 on v0

--- a/solution.py
+++ b/solution.py
@@ -93,7 +93,7 @@
     summed = jnp.sum(received, axis=0, keepdims=True)
     key_grad = summed[:, :, : local_kv * HD].astype(jnp.bfloat16)
     value_grad = summed[:, :, local_kv * HD :].astype(jnp.bfloat16)
-    gate_total = lax.psum(gate_acc, ("ctx", "tp"))
+    gate_total = lax.psum(lax.psum(gate_acc, "tp"), "ctx")
     term_count = tok_dev * lax.axis_size("ctx") * local_heads * lax.axis_size("tp") * HD
     gate_grad = ((1.0 - gate_value * gate_value) * gate_total / math.sqrt(term_count)).reshape(1)
     return (query_grad, key_grad, value_grad, gate_grad)

time: 887 us -> 947 us (1.068)
  the two profiles are of different devices: /device:TPU:1 before, /device:TPU:32 now
where the time goes in v1:
time: 947 us; the launch traced here: 945 us
  waiting for transfers between devices  595 us (63%)
  blocking collectives  203 us (21%)
  matrix products  61.8 us (7%)
  local copies, waits for them, and re-layouts  30.3 us (3%)
  other arithmetic  24.2 us (3%)
  between operations  16.7 us (2%)
    all_gather x1, waiting for transfers between devices, per_device(): lax.all_gather(image_keys, 'ctx', axis=0, tiled=True)  298 us
    all_gather x1, waiting for transfers between devices, per_device(): lax.all_gather(image_values, 'ctx', axis=0, tiled=True)  296 us
    psum x2, blocking collectives, per_device(): gate_total = lax.psum(lax.psum(gate_acc, 'tp'), 'ctx')  203 us
  transfers between devices with their start and end apart: 3, of which 2 were waited for; matrix products, arithmetic and copies ran while one was open for 1% of the time, Pallas kernels for 0%

profile of v1, /device:TPU:32, one launch (start us, length us, event | category | flops | bytes accessed | tf_op | source)
XLA Modules:
  0.0 945.3 jit_solution(2478909626626181388)
XLA Ops:
  10.9 2.0 top_k.11
  15.1 1.2 copy.35
  17.4 296.2 %all-gather.5.cloned.1.call-done = bf16[64,64,128]{2,1,0:T(8,128)(2,1)} async-done(((bf16[1,64,128]{2,1,0:T(8,128)(2,1)}), bf16[64,64,128]{2,1,0:T(8,128)(2,1)}) %all-gather.5.cloned.1.call-update) | async-done | bytes 1048592 | tf_op jit(solution)/shard_map/all_gather | solution.py:21
  313.6 1.9 gather_fusion.4
  315.5 297.8 %all-gather.3.cloned.1.call-done = bf16[64,64,128]{2,1,0:T(8,128)(2,1)} async-done(((bf16[1,64,128]{2,1,0:T(8,128)(2,1)}), bf16[64,64,128]{2,1,0:T(8,128)(2,1)}) %all-gather.3.cloned.1.call-update) | async-done | bytes 1048592 | tf_op jit(solution)/shard_map/all_gather | solution.py:20
  613.3 1.9 gather_fusion.3
  615.3 92.9 %while.17 = (s32[]{:T(128)}, f32[2048,1,128]{0,2,1:T(8,128)}, f32[2048,1,128]{0,2,1:T(8,128)}, f32[]{:T(128)}, bf16[8,256,1,128]{3,1,2,0:T(8,128)(2,1)}, /*index...) while((s32[]{:T(128)}, f32[2048,1,128]{0,2,1:T(8,128)}, ...), condition=%wide.region_7.9_spmd.clone, body=%wide.region_2.8_spmd.clone.sunk | while | flops 814710016 | bytes 48644448 | solution.py:77
  618.1 1.9 fusion.68
  620.7 1.4 fusion.69
  622.2 1.4 fusion.71
  624.7 1.3 fusion.70
  629.7 1.9 fusion.68
  632.3 1.4 fusion.69
  633.8 1.4 fusion.71
  636.3 1.3 fusion.70
  641.4 1.9 fusion.68
  644.0 1.4 fusion.69
  645.4 1.4 fusion.71
  647.9 1.3 fusion.70
  653.0 1.9 fusion.68
  655.6 1.4 fusion.69
  657.0 1.4 fusion.71
  659.5 1.3 fusion.70
  664.6 1.9 fusion.68
  667.2 1.4 fusion.69
  668.6 1.4 fusion.71
  671.1 1.3 fusion.70
  676.2 1.9 fusion.68
  678.8 1.4 fusion.69
  680.3 1.4 fusion.71
  682.7 1.3 fusion.70
  687.8 1.9 fusion.68
  690.4 1.4 fusion.69
  691.9 1.4 fusion.71
  694.4 1.3 fusion.70
  699.4 1.9 fusion.68
  702.0 1.4 fusion.69
  703.5 1.4 fusion.71
  706.0 1.3 fusion.70
  708.2 1.6 copy.40
  709.9 1.3 copy.41
  711.2 1.4 maximum_select_fusion
  712.7 2.5 broadcast_in_dim.68
  715.2 6.4 scatter_fusion
  721.5 8.2 all-to-all-start
  729.7 16.8 %psum.14 = f32[]{:T(128)} all-reduce(f32[]{:T(128)} %get-tuple-element.72), channel_id=1, replica_groups=mesh['ctx'=64,'tp'=8] {'tp'}, use_global_device_ids=true, to_apply=%region_10.12 | all-reduce | flops 1 | bytes 8 | tf_op jit(solution)/shard_map/psum | solution.py:96
  746.5 185.8 %psum.15 = f32[]{:T(128)} all-reduce(f32[]{:T(128)} %psum.14), channel_id=1, replica_groups=mesh['ctx'=64,'tp'=8] {'ctx'}, use_global_device_ids=true, to_apply=%region_11.13 | all-reduce | flops 1 | bytes 8 | tf_op jit(solution)/shard_map/psum | solution.py:96
  934.2 2.4 reduce_sum.36
  (182 shorter events, 46.8 us)
Async XLA Ops:
  7.2 6.5 copy-start
  7.2 9.2 copy-start.8
  7.2 306.5 %all-gather.5.cloned.1.call-start = ((), (), s32[]{:S(2)}) async-start(), calls=%async_computation.2 | async-start | bytes 1064960 | tf_op jit(solution)/shard_map/all_gather | solution.py:21
  7.9 605.4 %all-gather.3.cloned.1.call-start = ((), (), s32[]{:S(2)}) async-start(), calls=%async_computation.1 | async-start | bytes 1064960 | tf_op jit(solution)/shard_map/all_gather | solution.py:20
  615.3 1.4 copy-start.6
  620.7 1.4 copy-start.1
  622.2 2.5 copy-start.4
  623.6 2.4 copy-start.2
  623.6 3.4 copy-start.7
  627.0 1.4 copy-start.6
  632.3 1.5 copy-start.1
  633.8 2.5 copy-start.4
  635.2 2.4 copy-start.2
  635.2 3.4 copy-start.7
  637.6 1.0 copy-start.5
  638.6 1.4 copy-start.6
  644.0 1.5 copy-start.1
  645.4 2.5 copy-start.4
  646.8 2.4 copy-start.2
  646.8 3.4 copy-start.7
  650.2 1.4 copy-start.6
  655.6 1.5 copy-start.1
  657.0 2.5 copy-start.4
  658.4 2.4 copy-start.2
  658.4 3.4 copy-start.7
  661.8 1.4 copy-start.6
  667.2 1.5 copy-start.1
  668.6 2.5 copy-start.4
  670.0 2.4 copy-start.2
  670.0 3.4 copy-start.7
  673.4 1.4 copy-start.6
  678.8 1.5 copy-start.1
  680.3 2.5 copy-start.4
  681.6 2.4 copy-start.2
  681.7 3.4 copy-start.7
  685.0 1.4 copy-start.6
  690.4 1.5 copy-start.1
  691.9 2.5 copy-start.4
  693.3 2.4 copy-start.2
  693.3 3.4 copy-start.7
  696.6 1.4 copy-start.6
  702.0 1.5 copy-start.1
  703.5 2.5 copy-start.4
  704.9 2.4 copy-start.2
  704.9 3.4 copy-start.7
  708.2 1.6 copy-start.3
  721.5 210.8 %copy-start.9 = (bf16[8,256,1,128]{3,1,2,0:T(8,128)(2,1)S(1)}, bf16[8,256,1,128]{3,1,2,0:T(8,128)(2,1)}, u32[]{:S(2)}) copy-start(bf16[8,256,1,128]{3,1,2,0:T(8,128)(2,1)} %get-tuple-element.69) | copy-start | bytes 1572868
  721.5 212.7 %all-to-all-start = ((f32[64,64,256]{2,1,0:T(8,128)}), f32[64,64,256]{2,1,0:T(8,128)}, u32[]{:S(2)}, u32[]{:S(2)}) async-start(f32[64,64,256]{2,1,0:T(8,128)} %scatter_fusion), calls=%async_computation | async-start | bytes 8388608 | tf_op jit(solution)/shard_map/all_to_all | solution.py:92
  (7 other events, 6.9 us)
Sparse Core Ops, SparseCore 0:
  10.1 303.4 all-gather.4
  315.7 297.5 all-gather.2
